TPU v7x, 32 devices: a whole 2x2x4 slice. The times are simulated.
32 devices in a mesh: ctx: 8 (over y, x, core), tp: 4 (over z).
Axes of the slice: x: 2, y: 2, z: 4, core: 2. Of those that a mesh axis runs over, the one named last changes fastest.
Arguments:
- queries: bfloat16 [128, 8192], P('ctx', 'tp'), may hold values from -60 to 60
- rotated_keys: bfloat16 [1024, 1024], P('ctx', 'tp'), may hold values from -7 to 7
- value_rows: bfloat16 [1024, 1024], P('ctx', 'tp'), may hold values from -6 to 6
- span_order: int32 [16], replicated, may hold values from 0 to 15, each once
- targets: int32 [128], replicated, may hold values from 0 to 65535
- out_weight: bfloat16 [8192, 4, 8, 256], P('tp', None, 'ctx'), may hold values from -0.0625 to 0.0625
- residual: bfloat16 [128, 4, 8, 256], P(None, 'tp', 'ctx'), may hold values from -3 to 3
- norm_gain: float32 [4, 8, 256], P('tp', 'ctx'), may hold values from 0.5 to 1.5
- head_weight: bfloat16 [8192, 65536], P('tp', 'ctx'), may hold values from -2.253903 to 2.253903
Outputs:
- loss: float32 [], replicated
- grad_normed: bfloat16 [128, 8192], P('ctx', 'tp')
- grad_head: bfloat16 [8192, 65536], P('tp', 'ctx')
Inputs may be any that keep to these rules, and one draw needn't show every extreme that they name: `span_order`: each span number appears once.
All inputs are finite; a program needn't handle non-finite values.
Results may differ from a plain program's by a relative error of at most 0.012.
Values may be sent and summed in bfloat16 or wider, within the bound.
A program may use at most 128 MiB of HBM per device.

v0:
```python
import jax
import jax.numpy as jnp
from jax import lax
from jax.sharding import PartitionSpec as P

D = 8192
QUERY_HEADS = 64
KEY_VALUE_HEADS = 8
HEAD_SIZE = 128


EPSILON = 1e-05
MASKED = -1e30


def slot_positions(span_order, total_rows, slot_rows, span_rows, first_row):
    slots = jnp.arange(total_rows, dtype=jnp.int32)
    owners = slots // slot_rows
    table = owners[:, None] == jnp.arange(span_order.shape[0], dtype=jnp.int32)[None, :]
    starts = jnp.sum(jnp.where(table, span_order[None, :], 0), axis=1)
    return starts * span_rows + first_row + slots % slot_rows


def head_scores(grouped_queries, piece_keys):
    divided_keys = piece_keys.reshape(piece_keys.shape[0], -1, HEAD_SIZE)
    return jnp.einsum(
        "tkgd,skd->kgts", grouped_queries, divided_keys, preferred_element_type=jnp.float32
    ) * HEAD_SIZE ** (-0.5)


def score_stats(grouped_queries, mine, positions):

    def score_update(carry, piece, offset):
        visible = positions[None, :] <= mine[:, None]

        def score_accumulate(state):
            scores = jnp.where(visible, head_scores(grouped_queries, piece), MASKED)
            fresh = jnp.maximum(state[0], jnp.max(scores, axis=-1))
            added = jnp.sum(jnp.where(visible, jnp.exp(scores - fresh[..., None]), 0.0), axis=-1)
            return (fresh, added)

        return lax.cond(jnp.any(visible), score_accumulate, lambda state: state, carry)

    return score_update


def weighted_values(grouped_queries, mine, positions, peak, totals):

    def weighted_update(carry, pieces, offset):
        piece_keys, piece_values = pieces
        visible = positions[None, :] <= mine[:, None]

        def weighted_accumulate(state):
            scores = jnp.where(visible, head_scores(grouped_queries, piece_keys), MASKED)
            weights = jnp.where(visible, jnp.exp(scores - peak[..., None]), 0.0) / totals[..., None]
            divided_values = piece_values.reshape(piece_values.shape[0], -1, HEAD_SIZE)
            return jnp.einsum(
                "kgts,skd->tkgd",
                weights.astype(jnp.bfloat16),
                divided_values,
                preferred_element_type=jnp.float32,
            )

        return lax.cond(jnp.any(visible), weighted_accumulate, lambda state: state, carry)

    return weighted_update


def per_device(
    queries,
    rotated_keys,
    value_rows,
    span_order,
    targets,
    out_weight,
    residual,
    norm_gain,
    head_weight,
):
    tok_dev = rotated_keys.shape[0]
    q_dev = queries.shape[0]
    span_rows = tok_dev // 2
    q_span = q_dev // 2
    total_keys = tok_dev * lax.axis_size("ctx")
    total_rows = q_dev * lax.axis_size("ctx")
    positions = slot_positions(span_order, total_keys, span_rows, span_rows, 0)
    query_pos = slot_positions(span_order, total_rows, q_span, span_rows, span_rows - q_span)
    mine = lax.dynamic_slice_in_dim(query_pos, lax.axis_index("ctx") * q_dev, q_dev)
    group_size = QUERY_HEADS // KEY_VALUE_HEADS
    local_kv = rotated_keys.shape[1] // HEAD_SIZE
    grouped_queries = queries.reshape(q_dev, local_kv, group_size, HEAD_SIZE)
    start_stats = (
        jnp.full((local_kv, group_size, q_dev), MASKED, jnp.float32),
        jnp.zeros((local_kv, group_size, q_dev), jnp.float32),
    )
    start_acc = jnp.zeros((q_dev, local_kv, group_size, HEAD_SIZE), jnp.float32)
    stats_step = score_stats(grouped_queries, mine, positions)
    all_keys, all_values = (
        lax.all_gather(rotated_keys, "ctx", axis=0, tiled=True),
        lax.all_gather(value_rows, "ctx", axis=0, tiled=True),
    )
    peak, totals = stats_step(start_stats, all_keys, 0)
    value_step = weighted_values(grouped_queries, mine, positions, peak, totals)
    attn_acc = value_step(start_acc, (all_keys, all_values), 0)
    attn = attn_acc.astype(jnp.bfloat16).reshape(q_dev, -1)
    slice_width = out_weight.shape[3]
    out_local = out_weight.reshape(out_weight.shape[0], -1)
    mixed = jnp.dot(
        lax.all_gather(attn, "ctx", axis=0, tiled=True),
        out_local,
        preferred_element_type=jnp.float32,
    )
    mixed = lax.psum_scatter(
        mixed.reshape(total_rows, -1, slice_width), "tp", scatter_dimension=1, tiled=True
    )
    hidden = residual.reshape(total_rows, slice_width).astype(jnp.float32) + mixed.reshape(
        total_rows, slice_width
    )
    squares = lax.psum(jnp.sum(hidden * hidden, axis=1), ("ctx", "tp"))
    normed = (
        hidden * lax.rsqrt(squares / D + EPSILON)[:, None] * norm_gain.reshape(1, slice_width)
    ).astype(jnp.bfloat16)
    block = lax.all_gather(normed, "ctx", axis=1, tiled=True)
    vocab_width = head_weight.shape[1]
    first_col = lax.axis_index("ctx") * vocab_width
    logits = lax.psum_scatter(
        jnp.dot(block, head_weight, preferred_element_type=jnp.float32),
        "tp",
        scatter_dimension=0,
        tiled=True,
    )
    row_targets = lax.dynamic_slice_in_dim(
        targets, lax.axis_index("tp") * logits.shape[0], logits.shape[0]
    )
    columns = jnp.arange(vocab_width, dtype=jnp.int32)[None, :] + first_col
    target_hit = columns == row_targets[:, None]
    local_peak = jnp.max(logits, axis=1)
    picked = jnp.sum(jnp.where(target_hit, logits, 0.0), axis=1)
    row_peak = lax.pmax(local_peak, "ctx")
    expsum = jnp.sum(jnp.exp(logits - row_peak[:, None]), axis=1)
    expsum, picked = lax.psum((expsum, picked), "ctx")
    lse = row_peak + jnp.log(expsum)
    grad_logits = (jnp.exp(logits - lse[:, None]) - target_hit.astype(jnp.float32)).astype(
        jnp.bfloat16
    )
    loss_part = jnp.sum(lse - picked)
    loss = lax.psum(loss_part, "tp") / total_rows
    grad_logits = lax.all_gather(grad_logits, "tp", axis=0, tiled=True)
    grad_normed = lax.psum_scatter(
        lax.dot_general(
            grad_logits, head_weight, (((1,), (1,)), ((), ())), preferred_element_type=jnp.float32
        ),
        "ctx",
        scatter_dimension=0,
        tiled=True,
    ).astype(jnp.bfloat16)
    grad_head = lax.dot_general(
        block, grad_logits, (((0,), (0,)), ((), ())), preferred_element_type=jnp.float32
    ).astype(jnp.bfloat16)
    return (loss, grad_normed, grad_head)


def solution(mesh):
    placed = (
        P("ctx", "tp"),
        P("ctx", "tp"),
        P("ctx", "tp"),
        P(),
        P(),
        P("tp", None, "ctx", None),
        P(None, "tp", "ctx", None),
        P("tp", "ctx", None),
        P("tp", "ctx"),
    )
    return jax.shard_map(
        per_device,
        mesh=mesh,
        in_specs=placed,
        out_specs=(P(), P("ctx", "tp"), P("tp", "ctx")),
        check_vma=False,
    )
```

profile of v0, /device:TPU:1, one launch (start us, length us, event | category | flops | bytes accessed | tf_op | source)
XLA Modules:
  0.0 366.0 jit_solution(16360974205961195104)
XLA Ops:
  7.2 0.0 reduce-scatter.4.cloned.1.call-start
  7.2 0.7 select_reduce_fusion.2
  8.0 0.7 select_reduce_fusion.1
  8.7 0.1 dynamic_slice.6
  8.8 0.7 broadcast_compare_fusion
  10.2 0.9 copy.30
  11.1 11.5 %all_gather.15 = bf16[1024,256]{1,0:T(8,128)(2,1)S(1)} all-gather(bf16[128,256]{1,0:T(8,128)(2,1)} %param.14), channel_id=1, replica_groups=mesh['ctx'=8,'tp'=4] {'ctx'}, dimensions={0}, use_global_device_ids=true | all-gather | bytes 589824 | tf_op jit(solution)/shard_map/all_gather | solution.py:99
  22.6 9.5 %all_gather.16 = bf16[1024,256]{1,0:T(8,128)(2,1)S(1)} all-gather(bf16[128,256]{1,0:T(8,128)(2,1)} %param.15), channel_id=1, replica_groups=mesh['ctx'=8,'tp'=4] {'ctx'}, dimensions={0}, use_global_device_ids=true | all-gather | bytes 589824 | tf_op jit(solution)/shard_map/all_gather | solution.py:100
  32.1 2.1 conditional.2
  32.1 0.1 reshape.82
  32.2 0.4 fusion.42
  32.6 0.6 broadcast_maximum_fusion
  33.2 1.0 select_reduce_fusion
  34.2 1.6 conditional.3
  34.3 0.1 reshape.95
  34.4 0.1 reshape.84
  34.5 1.3 fusion.12
  35.9 9.2 %all_gather.17 = bf16[128,2048]{1,0:T(8,128)(2,1)S(1)} all-gather(bf16[16,2048]{1,0:T(8,128)(2,1)S(1)} %bitcast.67), channel_id=1, replica_groups=mesh['ctx'=8,'tp'=4] {'ctx'}, dimensions={0}, use_global_device_ids=true | all-gather | bytes 589824 | tf_op jit(solution)/shard_map/all_gather | solution.py:109
  45.1 5.2 %copy.32 = bf16[256,8,4,256]{3,1,2,0:T(8,128)(2,1)} copy(bf16[256,8,4,256]{3,2,1,0:T(4,128)(2,1)} %bitcast.64) | data formatting | bytes 8388608
  50.3 6.5 %copy.21 = bf16[1024,2048]{1,0:T(8,128)(2,1)} copy(bf16[1024,2048]{0,1:T(8,128)(2,1)} %bitcast.63) | data formatting | bytes 8388608 | tf_op jit(solution)/shard_map/dot_general | solution.py:108
  56.8 4.5 %fusion.30 = f32[128,4,256]{2,0,1:T(8,128)} fusion(bf16[4,256,2048]{2,1,0:T(8,128)(2,1)} %bitcast.62, bf16[128,2048]{1,0:T(8,128)(2,1)S(1)} %all_gather.17), kind=kOutput, calls=%fused_computation.36 | convolution fusion | flops 536870912 | bytes 5242880 | tf_op jit(solution)/shard_map/dot_general | solution.py:108
  61.4 0.0 reduce-scatter.4.cloned.1.call-update
  61.4 0.0 reduce-scatter.6.cloned.1.call-start
  61.4 19.8 %reduce-scatter.4.cloned.1.call-done = f32[128,1,256]{2,0,1:T(8,128)} async-done(((f32[128,4,256]{2,0,1:T(8,128)}), f32[128,1,256]{2,0,1:T(8,128)}) %reduce-scatter.4.cloned.1.call-update) | async-done | bytes 131088 | tf_op jit(solution)/shard_map/reduce_scatter | solution.py:113
  81.3 1.0 multiply_reduce_fusion
  82.3 39.5 %psum.28 = f32[128]{0:T(128)S(1)} all-reduce(f32[128]{0:T(128)S(1)} %multiply_reduce_fusion), channel_id=1, replica_groups=mesh['ctx'=8,'tp'=4] {'ctx','tp'}, use_global_device_ids=true, to_apply=%region_11.12 | all-reduce | flops 128 | bytes 1024 | tf_op jit(solution)/shard_map/psum | solution.py:119
  121.7 1.0 multiply_convert_fusion
  122.7 13.2 %all_gather.18 = bf16[128,2048]{1,0:T(8,128)(2,1)S(1)} all-gather(bf16[128,256]{1,0:T(8,128)(2,1)S(1)} %multiply_convert_fusion), channel_id=1, replica_groups=mesh['ctx'=8,'tp'=4] {'ctx'}, dimensions={1}, use_global_device_ids=true | all-gather | bytes 589824 | tf_op jit(solution)/shard_map/all_gather | solution.py:123
  135.9 17.1 %fusion.43 = f32[128,8192]{1,0:T(8,128)} fusion(bf16[128,2048]{1,0:T(8,128)(2,1)S(1)} %all_gather.18, bf16[2048,8192]{1,0:T(8,128)(2,1)} %param.21), kind=kOutput, calls=%fused_computation.71 | convolution fusion | flops 4294967296 | bytes 38273024 | tf_op jit(solution)/shard_map/dot_general | solution.py:127
  153.0 0.0 reduce-scatter.6.cloned.1.call-update
  153.0 0.0 all-gather.2.cloned.1.call-start
  153.1 0.6 copy-done.3
  153.6 0.1 dynamic_slice.7
  153.7 74.7 %reduce-scatter.6.cloned.1.call-done = f32[32,8192]{1,0:T(8,128)} async-done(((f32[128,8192]{1,0:T(8,128)}), f32[32,8192]{1,0:T(8,128)}) %reduce-scatter.6.cloned.1.call-update) | async-done | bytes 1048592 | tf_op jit(solution)/shard_map/reduce_scatter | solution.py:126
  228.4 1.4 reduce_max.18
  229.8 11.8 %pmax.7 = f32[32]{0:T(128)S(1)} all-reduce(f32[32]{0:T(128)S(1)} %reduce_max.18), channel_id=1, replica_groups=mesh['ctx'=8,'tp'=4] {'ctx'}, use_global_device_ids=true, to_apply=%region_14.15 | all-reduce | flops 32 | bytes 256 | tf_op jit(solution)/shard_map/pmax | solution.py:139
  241.6 1.6 fusion.27
  243.2 13.7 %all-reduce = (f32[32]{0:T(128)S(1)}, f32[32]{0:T(128)S(1)}) all-reduce(f32[32]{0:T(128)S(1)} %get-tuple-element.44, f32[32]{0:T(128)S(1)} %get-tuple-element.43), channel_id=1, replica_groups=mesh['ctx'=8,'tp'=4] {'ctx'}, use_global_device_ids=true, to_apply=%region_16.17 | all-reduce | flops 64 | bytes 512 | tf_op jit(solution)/shard_map/psum | solution.py:141
  256.9 0.6 subtract_reduce_fusion
  257.5 2.3 fusion.29
  259.8 0.0 all-gather.2.cloned.1.call-update
  259.8 0.0 reduce-scatter.8.cloned.1.call-start
  259.9 9.9 %psum.31 = f32[]{:T(128)} all-reduce(f32[]{:T(128)} %get-tuple-element.47), channel_id=1, replica_groups=mesh['ctx'=8,'tp'=4] {'tp'}, use_global_device_ids=true, to_apply=%region_20.21 | all-reduce | flops 1 | bytes 8 | tf_op jit(solution)/shard_map/psum | solution.py:147
  270.5 34.4 %all-gather.2.cloned.1.call-done = bf16[128,8192]{1,0:T(8,128)(2,1)} async-done(((bf16[32,8192]{1,0:T(8,128)(2,1)}), bf16[128,8192]{1,0:T(8,128)(2,1)}) %all-gather.2.cloned.1.call-update) | async-done | bytes 2097168 | tf_op jit(solution)/shard_map/all_gather | solution.py:148
  304.8 17.4 %fusion.44 = f32[128,2048]{1,0:T(8,128)} fusion(bf16[128,8192]{1,0:T(8,128)(2,1)} %all-gather.2.cloned.1.call-done, bf16[2048,8192]{1,0:T(8,128)(2,1)} %param.21), kind=kOutput, calls=%fused_computation.72 | convolution fusion | flops 4294967296 | bytes 36700160 | tf_op jit(solution)/shard_map/dot_general | solution.py:150
  322.3 14.3 %convolution_convert_fusion = bf16[2048,8192]{1,0:T(8,128)(2,1)} fusion(bf16[128,2048]{1,0:T(8,128)(2,1)S(1)} %all_gather.18, bf16[128,8192]{1,0:T(8,128)(2,1)S(1)} %copy-done), kind=kOutput, calls=%fused_computation.29 | convolution fusion | flops 4311744512 | bytes 36175872 | tf_op jit(solution)/shard_map/dot_general | solution.py:157
  336.6 20.2 %reduce-scatter.8.cloned.1.call-done = f32[16,2048]{1,0:T(8,128)} async-done(((f32[128,2048]{1,0:T(8,128)}), f32[16,2048]{1,0:T(8,128)}) %reduce-scatter.8.cloned.1.call-update) | async-done | bytes 131088 | tf_op jit(solution)/shard_map/reduce_scatter | solution.py:149
  356.8 1.5 convert_element_type.38
  (16 shorter events, 0.1 us)
Async XLA Ops:
  7.2 74.1 %reduce-scatter.4.cloned.1.call-start = ((), (), s32[]{:S(2)}) async-start(), calls=%async_computation.3 | async-start | bytes 655360 | tf_op jit(solution)/shard_map/reduce_scatter | solution.py:113
  56.8 24.4 %copy-start.1 = (bf16[128,1,1,256]{3,0,2,1:T(8,128)(2,1)S(1)}, bf16[128,1,1,256]{3,0,2,1:T(8,128)(2,1)}, u32[]{:S(2)}) copy-start(bf16[128,1,1,256]{3,0,2,1:T(8,128)(2,1)} %param.19) | copy-start | bytes 196612
  56.8 64.9 %copy-start.2 = (f32[1,1,256]{2,1,0:T(1,128)S(1)}, f32[1,1,256]{2,1,0:T(1,128)}, u32[]{:S(2)}) copy-start(f32[1,1,256]{2,1,0:T(1,128)} %param.20) | copy-start | bytes 3076
  61.4 167.0 %reduce-scatter.6.cloned.1.call-start = ((), (), s32[]{:S(2)}) async-start(), calls=%async_computation.4 | async-start | bytes 5242880 | tf_op jit(solution)/shard_map/reduce_scatter | solution.py:126
  153.0 0.7 copy-start.3
  153.0 151.8 %all-gather.2.cloned.1.call-start = ((), (), s32[]{:S(2)}) async-start(), calls=%async_computation.5 | async-start | bytes 2621440 | tf_op jit(solution)/shard_map/all_gather | solution.py:148
  259.8 97.0 %reduce-scatter.8.cloned.1.call-start = ((), (), s32[]{:S(2)}) async-start(), calls=%async_computation.6 | async-start | bytes 1179648 | tf_op jit(solution)/shard_map/reduce_scatter | solution.py:149
  304.8 17.4 %copy-start = (bf16[128,8192]{1,0:T(8,128)(2,1)S(1)}, bf16[128,8192]{1,0:T(8,128)(2,1)}, u32[]{:S(2)}) copy-start(bf16[128,8192]{1,0:T(8,128)(2,1)} %all-gather.2.cloned.1.call-done) | copy-start | bytes 6291460
Sparse Core Ops, SparseCore 0:
  61.5 19.7 reduce-scatter.3
  153.1 75.2 reduce-scatter.5
  260.0 44.8 all-gather.1
  322.4 34.3 reduce-scatter.7
where the time goes:
time: 368 us; the launch traced here: 366 us
  waiting for transfers between devices  149 us (40%)
  blocking collectives  118 us (32%)
  matrix products  55 us (15%)
  between operations  16.3 us (4%)
  local copies, waits for them, and re-layouts  13.7 us (4%)
  other arithmetic  13.3 us (4%)
    reduce_scatter x1, waiting for transfers between devices, per_device(): lax.psum_scatter(jnp.dot(block, head_weight, preferred_element_type=jnp.f...  74.7 us
    psum x1, blocking collectives, per_device(): squares = lax.psum(jnp.sum(hidden * hidden, axis=1), ('ctx', 'tp'))  39.5 us
    all_gather x1, waiting for transfers between devices, per_device(): grad_logits = lax.all_gather(grad_logits, 'tp', axis=0, tiled=True)  34.4 us
    reduce_scatter x1, waiting for transfers between devices, per_device(): lax.psum_scatter(lax.dot_general(grad_logits, head_weight, (((1,), (1,)),...  20.2 us
    reduce_scatter x1, waiting for transfers between devices, per_device(): lax.psum_scatter(mixed.reshape(total_rows, -1, slice_width), 'tp', scatte...  19.8 us
    dot_general x1, matrix products, per_device(): lax.dot_general(grad_logits, head_weight, (((1,), (1,)), ((), ())), prefe...  17.4 us
    dot_general x1, matrix products, per_device(): jnp.dot(block, head_weight, preferred_element_type=jnp.float32)  17.1 us
    dot_general x1, matrix products, per_device(): lax.dot_general(block, grad_logits, (((0,), (0,)), ((), ())), preferred_e...  14.3 us
  transfers between devices with their start and end apart: 4, of which 4 were waited for; matrix products, arithmetic and copies ran while one was open for 4% of the time, Pallas kernels for 0%

commit v1 on v0

--- a/solution.py
+++ b/solution.py
@@ -1,6 +1,10 @@
+import functools
+
 import jax
 import jax.numpy as jnp
 from jax import lax
+from jax.experimental import pallas as pl
+from jax.experimental.pallas import tpu as pltpu
 from jax.sharding import PartitionSpec as P
 
 D = 8192
@@ -160,6 +164,541 @@
     return (loss, grad_normed, grad_head)
 
 
+MESH = pl.DeviceIdType.MESH
+F32 = jnp.float32
+BF16 = jnp.bfloat16
+
+
+def fused_kernel(
+    nc,
+    chunk,
+    q_ref,
+    k_ref,
+    v_ref,
+    kpos_ref,
+    qpos_ref,
+    target_ref,
+    wo_hbm,
+    resid_ref,
+    gain_ref,
+    w_hbm,
+    loss_ref,
+    gn_ref,
+    block_ref,
+    gl_ref,
+    w,
+    wo,
+    kv_all,
+    attn,
+    mix_out,
+    mix_in,
+    square_tp,
+    square_ctx,
+    norm_all,
+    part_out,
+    pair_in,
+    far_in,
+    logit,
+    pack,
+    stat,
+    loss_all,
+    hidden_grad,
+    grad_out,
+    grad_in,
+    w_sem,
+    wo_sem,
+    gather_send,
+    gather_recv,
+    mix_sem,
+    square_sem,
+    cross_sem,
+    part_send,
+    part_recv,
+    stat_sem,
+    loss_sem,
+    share_send,
+    share_recv,
+    grad_sem,
+):
+    tp = 4
+    c = lax.axis_index("ctx")
+    t = lax.axis_index("tp")
+    chip, core = c // 2, c % 2
+    chips = nc // 2
+    mate = chip * 2 + 1 - core
+    rows = gl_ref.shape[0]
+    own = rows // tp
+    vocab = gl_ref.shape[1]
+    chunks = vocab // chunk
+    q_dev = q_ref.shape[0]
+    width = gain_ref.shape[1]
+    depth = w.shape[0]
+    tile = 256
+
+    def remote(src, dst, send, recv, where):
+        return pltpu.make_async_remote_copy(
+            src_ref=src, dst_ref=dst, send_sem=send, recv_sem=recv, device_id=where, device_id_type=MESH
+        )
+
+    def w_copy(j):
+        span = pl.ds(pl.multiple_of(j * chunk, chunk), chunk)
+        return pltpu.make_async_copy(w_hbm.at[:, span], w.at[:, span], w_sem.at[j])
+
+    wo_copy = pltpu.make_async_copy(wo_hbm, wo, wo_sem)
+    wo_copy.start()
+
+    barrier = pltpu.get_barrier_semaphore()
+    for d in range(1, nc):
+        pl.semaphore_signal(barrier, inc=1, device_id=(lax.rem(c + d, nc), t), device_id_type=MESH)
+    for d in range(1, tp):
+        pl.semaphore_signal(barrier, inc=1, device_id=(c, lax.rem(t + d, tp)), device_id_type=MESH)
+    pl.semaphore_wait(barrier, nc + tp - 2)
+
+    def gather(buf, at, stage):
+        def send(idx, d, to):
+            return remote(at(buf, idx), at(buf, idx), gather_send.at[stage, d], gather_recv.at[stage, d], (to, t))
+
+        first = [send(c, 0, mate)]
+        for d in range(1, chips):
+            first.append(send(c, d, lax.rem(chip + d, chips) * 2 + core))
+        for copy in first[1:] + first[:1]:
+            copy.start()
+        passed = []
+        for d in range(1, chips):
+            first[d].wait_recv()
+            idx = lax.rem(chip + chips - d, chips) * 2 + core
+            passed.append(send(idx, chips + d, mate))
+            passed[-1].start()
+        first[0].wait_recv()
+        for copy in passed:
+            copy.wait_recv()
+        for copy in first + passed:
+            copy.wait_send()
+
+    tok_dev = k_ref.shape[0]
+    kv_all[c, pl.ds(0, tok_dev), :] = k_ref[...]
+    kv_all[c, pl.ds(tok_dev, tok_dev), :] = v_ref[...]
+    gather(kv_all, lambda buf, idx: buf.at[idx], 0)
+    for j in range(chunks):
+        w_copy(j).start()
+
+    local_kv = k_ref.shape[1] // HEAD_SIZE
+    group = QUERY_HEADS // KEY_VALUE_HEADS
+    visible = kpos_ref[...] <= qpos_ref[...]
+    pieces = []
+    for k in range(local_kv):
+        lanes = pl.ds(k * HEAD_SIZE, HEAD_SIZE)
+        heads = [
+            q_ref[:, (k * group + g) * HEAD_SIZE : (k * group + g + 1) * HEAD_SIZE] for g in range(group)
+        ]
+        keys = kv_all[:, pl.ds(0, tok_dev), lanes].reshape(nc * tok_dev, HEAD_SIZE)
+        values = kv_all[:, pl.ds(tok_dev, tok_dev), lanes].reshape(nc * tok_dev, HEAD_SIZE)
+        scores = lax.dot_general(
+            jnp.concatenate(heads, axis=0), keys, (((1,), (1,)), ((), ())), preferred_element_type=F32
+        ) * HEAD_SIZE ** (-0.5)
+        scores = jnp.where(visible, scores, MASKED)
+        weights = jnp.exp(scores - jnp.max(scores, axis=1, keepdims=True))
+        weights = weights / jnp.sum(weights, axis=1, keepdims=True)
+        mixed = jnp.dot(weights.astype(BF16), values, preferred_element_type=F32).astype(BF16)
+        for g in range(group):
+            pieces.append(mixed[g * q_dev : (g + 1) * q_dev])
+    attn[pl.ds(pl.multiple_of(c * q_dev, 16), q_dev), :] = jnp.concatenate(pieces, axis=1)
+    gather(attn, lambda buf, idx: buf.at[pl.ds(pl.multiple_of(idx * q_dev, 16), q_dev), :], 1)
+
+    wo_copy.wait()
+
+    def project(owner):
+        columns = pl.ds(pl.multiple_of(owner * width, width), width)
+        return jnp.dot(attn[...], wo[:, columns], preferred_element_type=F32)
+
+    mixes = []
+    for d in range(1, tp):
+        owner = lax.rem(t + d, tp)
+        mix_out[d - 1] = project(owner).astype(BF16)
+        copy = remote(
+            mix_out.at[d - 1], mix_in.at[d - 1], mix_sem.at[0, d - 1], mix_sem.at[1, d - 1], (c, owner)
+        )
+        copy.start()
+        mixes.append(copy)
+    hidden = resid_ref[...].astype(F32) + project(t)
+    for copy in mixes:
+        copy.wait()
+    for d in range(1, tp):
+        hidden = hidden + mix_in[d - 1].astype(F32)
+
+    squares = jnp.sum(hidden * hidden, axis=1, keepdims=True)
+    square_tp[0] = jnp.broadcast_to(squares, (rows, rows)).T[0:8]
+    copies = []
+    for d in range(1, tp):
+        copy = remote(
+            square_tp.at[0], square_tp.at[d], square_sem.at[0, d], square_sem.at[1, d], (c, lax.rem(t + d, tp))
+        )
+        copy.start()
+        copies.append(copy)
+    for copy in copies:
+        copy.wait()
+    square_ctx[0] = square_tp[0] + square_tp[1] + square_tp[2] + square_tp[3]
+    copies = []
+    for d in range(1, nc):
+        copy = remote(
+            square_ctx.at[0], square_ctx.at[d], cross_sem.at[0, d], cross_sem.at[1, d], (lax.rem(c + d, nc), t)
+        )
+        copy.start()
+        copies.append(copy)
+    for copy in copies:
+        copy.wait()
+    total = square_ctx[0]
+    for d in range(1, nc):
+        total = total + square_ctx[d]
+    scale = lax.rsqrt(total / D + EPSILON)
+    scale = jnp.broadcast_to(scale[0:1], (rows, rows)).T
+    scale = jnp.concatenate([scale] * (width // rows), axis=1)
+    norm_all[c] = (hidden * scale * gain_ref[...]).astype(BF16)
+    gather(norm_all, lambda buf, idx: buf.at[idx], 2)
+    for i in range(nc):
+        block_ref[:, i * width : (i + 1) * width] = norm_all[i]
+
+    inner = jnp.logical_or(t == 1, t == 2)
+    pair_mate = t + 1 - 2 * (t % 2)
+    first_far = 2 - 2 * (t // 2)
+    rest = rows - own
+    rest_at = jnp.where(t < 2, own, 0)
+    far_in_rest = jnp.where(t < 2, own, 0)
+    own_in_rest = jnp.where(t < 2, 0, 2 * own)
+
+    def columns_of(j):
+        return pl.ds(pl.multiple_of(j * chunk, chunk), chunk)
+
+    def end_copy(j):
+        cols = columns_of(j)
+        return remote(
+            part_out.at[pl.ds(pl.multiple_of(jnp.where(t < 2, own, 0), 16), rest), cols],
+            pair_in.at[pl.ds(0, rest), cols],
+            part_send.at[0, j],
+            part_recv.at[0, j],
+            (c, pair_mate),
+        )
+
+    def inner_copy(j):
+        cols = columns_of(j)
+        return remote(
+            part_out.at[pl.ds(pl.multiple_of(pair_mate * own, 16), own), cols],
+            pair_in.at[pl.ds(0, own), cols],
+            part_send.at[0, j],
+            part_recv.at[0, j],
+            (c, pair_mate),
+        )
+
+    def far_copy(j, i):
+        cols = columns_of(j)
+        owner = first_far + i
+        return remote(
+            part_out.at[pl.ds(pl.multiple_of(owner * own, 16), own), cols],
+            far_in.at[:, cols],
+            part_send.at[1 + i, j],
+            part_recv.at[1, j],
+            (c, owner),
+        )
+
+    own_rows = pl.ds(pl.multiple_of(t * own, 16), own)
+
+    @pl.loop(0, chunks)
+    def _(j):
+        w_copy(j).wait()
+
+        @pl.loop(0, chunk // tile)
+        def _(i):
+            cols = pl.ds(pl.multiple_of(j * chunk + i * tile, tile), tile)
+            hidden_grad[:, 0:tile] = jnp.dot(block_ref[...], w[:, cols], preferred_element_type=F32)
+            part_out[:, cols] = hidden_grad[:, 0:tile].astype(BF16)
+            logit[:, cols] = hidden_grad[own_rows, 0:tile]
+
+        @pl.when(inner)
+        def _():
+            inner_copy(j).start()
+
+        @pl.when(jnp.logical_not(inner))
+        def _():
+            end_copy(j).start()
+
+    @pl.when(inner)
+    def _():
+        @pl.loop(0, chunks)
+        def _(j):
+            cols = columns_of(j)
+            end_copy(j).wait_recv()
+            far = pl.ds(pl.multiple_of(first_far * own, 16), 2 * own)
+            total = part_out[far, cols].astype(F32) + pair_in[
+                pl.ds(pl.multiple_of(far_in_rest, 16), 2 * own), cols
+            ].astype(F32)
+            part_out[far, cols] = total.astype(BF16)
+            far_copy(j, 0).start()
+            far_copy(j, 1).start()
+            logit[:, cols] += pair_in[pl.ds(pl.multiple_of(own_in_rest, 16), own), cols].astype(F32)
+
+    first_col = c * vocab
+    hits = target_ref[own_rows, :] - first_col
+
+    def column_ids(j):
+        return lax.broadcasted_iota(jnp.int32, (own, chunk), 1) + j * chunk
+
+    def settle(j, state):
+        peak, sums, picked = state
+        cols = columns_of(j)
+
+        @pl.when(jnp.logical_not(inner))
+        def _():
+            inner_copy(j).wait_recv()
+            logit[:, cols] += pair_in[0:own, cols].astype(F32)
+
+        far_copy(j, 0).wait_recv()
+        values = logit[:, cols] + far_in[:, cols].astype(F32)
+        logit[:, cols] = values
+        fresh = jnp.maximum(peak, jnp.max(values, axis=1, keepdims=True))
+        sums = sums * jnp.exp(peak - fresh) + jnp.sum(jnp.exp(values - fresh), axis=1, keepdims=True)
+        picked = picked + jnp.sum(jnp.where(column_ids(j) == hits, values, 0.0), axis=1, keepdims=True)
+        return fresh, sums, picked
+
+    zero = jnp.zeros((own, 1), F32)
+    peak, sums, picked = lax.fori_loop(0, chunks, settle, (zero + MASKED, zero, zero))
+
+    lane = lax.broadcasted_iota(jnp.int32, (own, 128), 1)
+    pack[...] = jnp.where(lane == 0, peak, jnp.where(lane == 1, sums, picked))
+    copies = []
+    for d in range(1, nc):
+        copy = remote(pack, stat.at[c], stat_sem.at[0, d], stat_sem.at[1, d], (lax.rem(c + d, nc), t))
+        copy.start()
+        copies.append(copy)
+    stat[c] = pack[...]
+    for copy in copies:
+        copy.wait()
+    top = stat[0][:, 0:1]
+    for i in range(1, nc):
+        top = jnp.maximum(top, stat[i][:, 0:1])
+    sums, picked = zero, zero
+    for i in range(nc):
+        sums = sums + stat[i][:, 1:2] * jnp.exp(stat[i][:, 0:1] - top)
+        picked = picked + stat[i][:, 2:3]
+    lse = top + jnp.log(sums)
+
+    loss_all[t] = jnp.broadcast_to(jnp.sum(lse - picked, axis=0, keepdims=True), (8, 128))
+    losses = []
+    for d in range(1, tp):
+        copy = remote(
+            loss_all.at[t], loss_all.at[t], loss_sem.at[0, d], loss_sem.at[1, d], (c, lax.rem(t + d, tp))
+        )
+        copy.start()
+        losses.append(copy)
+
+    def share(j, source, step):
+        place = gl_ref.at[pl.ds(pl.multiple_of(source * own, 16), own), columns_of(j)]
+        to = jnp.where(step > 0, jnp.minimum(t + 1, tp - 1), jnp.maximum(t - 1, 0))
+        return remote(
+            place, place, share_send.at[(step > 0) * tp + source, j], share_recv.at[source, j], (c, to)
+        )
+
+    @pl.loop(0, chunks)
+    def _(j):
+        cols = columns_of(j)
+        grads = jnp.exp(logit[:, cols] - lse) - (column_ids(j) == hits).astype(F32)
+        gl_ref[own_rows, cols] = grads.astype(BF16)
+
+        @pl.when(t < tp - 1)
+        def _():
+            share(j, t, 1).start()
+
+        @pl.when(t > 0)
+        def _():
+            share(j, t, 0).start()
+
+    hidden_grad[...] = jnp.zeros_like(hidden_grad)
+
+    @pl.loop(0, chunks)
+    def _(j):
+        for far in range(1, tp):
+
+            @pl.when(t - far >= 0)
+            def _():
+                share(j, t - far, 1).wait_recv()
+
+                @pl.when(t < tp - 1)
+                def _():
+                    share(j, t - far, 1).start()
+
+            @pl.when(t + far < tp)
+            def _():
+                share(j, t + far, 0).wait_recv()
+
+                @pl.when(t > 0)
+                def _():
+                    share(j, t + far, 0).start()
+
+        @pl.loop(0, depth // tile)
+        def _(i):
+            cols = pl.ds(pl.multiple_of(i * tile, tile), tile)
+            hidden_grad[:, cols] += lax.dot_general(
+                gl_ref[:, columns_of(j)],
+                w[cols, columns_of(j)],
+                (((1,), (1,)), ((), ())),
+                preferred_element_type=F32,
+            )
+
+    grad_out[...] = hidden_grad[...].astype(BF16)
+    copies = []
+    for d in range(1, nc):
+        to = lax.rem(c + d, nc)
+        copy = remote(
+            grad_out.at[pl.ds(pl.multiple_of(to * q_dev, 16), q_dev), :],
+            grad_in.at[d - 1],
+            grad_sem.at[0, d],
+            grad_sem.at[1, d],
+            (to, t),
+        )
+        copy.start()
+        copies.append(copy)
+
+    @pl.loop(0, chunks)
+    def _(j):
+        @pl.when(inner)
+        def _():
+            inner_copy(j).wait_send()
+            far_copy(j, 0).wait_send()
+            far_copy(j, 1).wait_send()
+
+        @pl.when(jnp.logical_not(inner))
+        def _():
+            end_copy(j).wait_send()
+
+        @pl.when(t < tp - 1)
+        def _():
+            share(j, t, 1).wait_send()
+            for far in range(1, tp):
+
+                @pl.when(t - far >= 0)
+                def _():
+                    share(j, t - far, 1).wait_send()
+
+        @pl.when(t > 0)
+        def _():
+            share(j, t, 0).wait_send()
+            for far in range(1, tp):
+
+                @pl.when(t + far < tp)
+                def _():
+                    share(j, t + far, 0).wait_send()
+
+    for copy in losses:
+        copy.wait()
+    loss_ref[...] = (loss_all[0] + loss_all[1] + loss_all[2] + loss_all[3]) / rows
+
+    result = hidden_grad[pl.ds(pl.multiple_of(c * q_dev, 16), q_dev), :]
+    for copy in copies:
+        copy.wait()
+    for d in range(1, nc):
+        result = result + grad_in[d - 1].astype(F32)
+    gn_ref[...] = result.astype(BF16)
+
+
+def fused_per_device(
+    queries,
+    rotated_keys,
+    value_rows,
+    span_order,
+    targets,
+    out_weight,
+    residual,
+    norm_gain,
+    head_weight,
+):
+    nc, tp = lax.axis_size("ctx"), lax.axis_size("tp")
+    tok_dev, kv_width = rotated_keys.shape
+    q_dev, q_width = queries.shape
+    span_rows, q_span = tok_dev // 2, q_dev // 2
+    rows = q_dev * nc
+    own = rows // tp
+    slice_width = out_weight.shape[3]
+    depth, vocab = head_weight.shape
+    chunk = min(1024, vocab)
+    chunks = vocab // chunk
+    kpos = slot_positions(span_order, tok_dev * nc, span_rows, span_rows, 0)
+    qpos = slot_positions(span_order, rows, q_span, span_rows, span_rows - q_span)
+    mine = lax.dynamic_slice_in_dim(qpos, lax.axis_index("ctx") * q_dev, q_dev)
+    mine = jnp.tile(mine, QUERY_HEADS // KEY_VALUE_HEADS)[:, None]
+    vmem = pl.BlockSpec(memory_space=pltpu.VMEM)
+    hbm = pl.BlockSpec(memory_space=pl.ANY)
+    dma = pltpu.SemaphoreType.DMA
+    loss, grad_normed, block, grad_logits = pl.pallas_call(
+        functools.partial(fused_kernel, nc, chunk),
+        out_shape=(
+            jax.ShapeDtypeStruct((8, 128), F32),
+            jax.ShapeDtypeStruct((q_dev, depth), BF16),
+            jax.ShapeDtypeStruct((rows, depth), BF16),
+            jax.ShapeDtypeStruct((rows, vocab), BF16),
+        ),
+        in_specs=[vmem] * 6 + [hbm, vmem, vmem, hbm],
+        out_specs=(vmem,) * 4,
+        scratch_shapes=[
+            pltpu.VMEM((depth, vocab), BF16),
+            pltpu.VMEM((q_width, tp * slice_width), BF16),
+            pltpu.VMEM((nc, 2 * tok_dev, kv_width), BF16),
+            pltpu.VMEM((rows, q_width), BF16),
+            pltpu.VMEM((tp - 1, rows, slice_width), BF16),
+            pltpu.VMEM((tp - 1, rows, slice_width), BF16),
+            pltpu.VMEM((tp, 8, rows), F32),
+            pltpu.VMEM((nc, 8, rows), F32),
+            pltpu.VMEM((nc, rows, slice_width), BF16),
+            pltpu.VMEM((rows, vocab), BF16),
+            pltpu.VMEM((rows - own, vocab), BF16),
+            pltpu.VMEM((own, vocab), BF16),
+            pltpu.VMEM((own, vocab), F32),
+            pltpu.VMEM((own, 128), F32),
+            pltpu.VMEM((nc, own, 128), F32),
+            pltpu.VMEM((tp, 8, 128), F32),
+            pltpu.VMEM((rows, depth), F32),
+            pltpu.VMEM((rows, depth), BF16),
+            pltpu.VMEM((nc - 1, q_dev, depth), BF16),
+            dma((chunks,)),
+            dma,
+            dma((3, nc)),
+            dma((3, nc)),
+            dma((2, tp - 1)),
+            dma((2, tp)),
+            dma((2, nc)),
+            dma((3, chunks)),
+            dma((2, chunks)),
+            dma((2, nc)),
+            dma((2, tp)),
+            dma((2 * tp, chunks)),
+            dma((tp, chunks)),
+            dma((2, nc)),
+        ],
+        compiler_params=pltpu.CompilerParams(
+            collective_id=0, has_side_effects=True, vmem_limit_bytes=58 * 1024 * 1024
+        ),
+    )(
+        queries,
+        rotated_keys,
+        value_rows,
+        kpos[None, :],
+        mine,
+        targets[:, None],
+        out_weight.reshape(q_width, -1),
+        residual.reshape(rows, slice_width),
+        norm_gain.reshape(1, slice_width),
+        head_weight,
+    )
+    grad_head = lax.dot_general(
+        block, grad_logits, (((0,), (0,)), ((), ())), preferred_element_type=jnp.float32
+    ).astype(jnp.bfloat16)
+    return (loss[0, 0], grad_normed, grad_head)
+
+
+def fits_kernel(mesh):
+    nc, tp = mesh.shape["ctx"], mesh.shape["tp"]
+    width = D // (nc * tp)
+    return tp == 4 and nc % 2 == 0 and width % 128 == 0
+
+
 def solution(mesh):
     placed = (
         P("ctx", "tp"),
@@ -173,7 +712,7 @@
         P("tp", "ctx"),
     )
     return jax.shard_map(
-        per_device,
+        fused_per_device if fits_kernel(mesh) else per_device,
         mesh=mesh,
         in_specs=placed,
         out_specs=(P(), P("ctx", "tp"), P("tp", "ctx")),

time: 368 us -> 188 us (0.51)
  Pallas kernels: 0 us -> 160 us
  waiting for transfers between devices: 149 us -> 0 us
  blocking collectives: 118 us -> 0 us
  matrix products: 55 us -> 16.2 us
  between operations: 16.3 us -> 0.67 us
  other arithmetic: 13.3 us -> 2.09 us
  local copies, waits for them, and re-layouts: 13.7 us -> 9.23 us
    pallas_call x0 -> x1, Pallas kernels: none -> 160 us  [fused_per_device(): pl.pallas_call(functools.partial(fused_kernel, nc, chunk), out_shape=(jax...]
    reduce_scatter x3 -> x0, waiting for transfers between devices: 115 us -> none  [the longest x1 74.7 us: per_device(): lax.psum_scatter(jnp.dot(block, head_weight, preferred_element_type=jnp.f...]
    psum x3 -> x0, blocking collectives: 63 us -> none  [the longest x1 39.5 us: per_device(): squares = lax.psum(jnp.sum(hidden * hidden, axis=1), ('ctx', 'tp'))]
    all_gather x4 -> x0, blocking collectives: 43.4 us -> none  [the longest x1 13.2 us: per_device(): block = lax.all_gather(normed, 'ctx', axis=1, tiled=True)]
    dot_general x6 -> x1, matrix products: 55 us -> 16.2 us  [fused_per_device(): lax.dot_general(block, grad_logits, (((0,), (0,)), ((), ())), preferred_e...]
    all_gather x1 -> x0, waiting for transfers between devices: 34.4 us -> none  [per_device(): grad_logits = lax.all_gather(grad_logits, 'tp', axis=0, tiled=True)]
    pmax x1 -> x0, blocking collectives: 11.8 us -> none  [per_device(): row_peak = lax.pmax(local_peak, 'ctx')]
    dot_general x1 -> x0, local copies, waits for them, and re-layouts: 6.49 us -> none  [per_device(): jnp.dot(lax.all_gather(attn, 'ctx', axis=0, tiled=True), out_local, prefe...]
  transfers between devices with their start and end apart: 4 -> 0, of which waited for: 4 -> 0; matrix products, arithmetic and copies ran while one was open for 4% -> 0% of each run, Pallas kernels for 0% -> 0%
where the time goes in v1:
time: 188 us
  Pallas kernels  160 us (85%)
  matrix products  16.2 us (9%)
  local copies, waits for them, and re-layouts  9.23 us (5%)
  other arithmetic  2.09 us (1%)
    pallas_call x1, Pallas kernels, fused_per_device(): pl.pallas_call(functools.partial(fused_kernel, nc, chunk), out_shape=(jax...  160 us
    dot_general x1, matrix products, fused_per_device(): lax.dot_general(block, grad_logits, (((0,), (0,)), ((), ())), preferred_e...  16.2 us
    unnamed x4, local copies, waits for them, and re-layouts  5.88 us

profile of v1, /device:TPU:1, one launch (start us, length us, event | category | flops | bytes accessed | tf_op | source)
XLA Modules:
  0.0 187.9 jit_solution(6925840094755941922)
XLA Ops:
  0.6 0.7 select_reduce_fusion.1
  1.4 0.1 dynamic_slice.3
  1.5 0.7 select_reduce_fusion
  2.2 0.6 fusion.kpos_ref
  2.8 0.7 broadcast_in_dim_tile.4.qpos_ref
  3.5 1.4 copy.15.target_ref
  4.9 5.2 %copy.16 = bf16[256,8,4,256]{3,1,2,0:T(8,128)(2,1)} copy(bf16[256,8,4,256]{3,2,1,0:T(4,128)(2,1)} %bitcast.12) | data formatting | bytes 8388608
  10.2 159.7 %shard_map.112 = (f32[8,128]{1,0:T(8,128)}, bf16[16,2048]{1,0:T(8,128)(2,1)}, bf16[128,2048]{1,0:T(8,128)(2,1)}, bf16[128,8192]{1,0:T(8,128)(2,1)}) custom-call(bf16[16,2048]{1,0:T(8,128)(2,1)} %q_ref.1, bf16[128,256]{1,0:T(8,128)(2,1)} %k_ref.1, bf16[128,256]{1,0:T(8,128)(2,1)} %v_ref.1, s32[1,1024]{1,0:T(1,128)} %fusion.kpos_ref, ...), custom_call_target="tpu_custom_call" | custom-call | tf_op jit(solution)/shard_map/pallas_call | solution.py:630
  169.9 1.2 slice.3
  171.1 0.0 copy-start
  171.1 16.2 %convolution_convert_fusion = bf16[2048,8192]{1,0:T(8,128)(2,1)} fusion(bf16[128,2048]{1,0:T(8,128)(2,1)} %get-tuple-element.9, bf16[128,8192]{1,0:T(8,128)(2,1)} %get-tuple-element.10), kind=kOutput, calls=%fused_computation | convolution fusion | flops 4311744512 | bytes 36175872 | tf_op jit(solution)/shard_map/dot_general | solution.py:690
  187.3 0.0 copy-done
  187.3 0.6 copy.18
  (5 shorter events, 0.0 us)
Async XLA Ops:
  171.1 16.2 %copy-start = (bf16[16,2048]{1,0:T(8,128)(2,1)S(1)}, bf16[16,2048]{1,0:T(8,128)(2,1)}, u32[]{:S(2)}) copy-start(bf16[16,2048]{1,0:T(8,128)(2,1)} %get-tuple-element.15) | copy-start | bytes 196612

commit v2 on v1

--- a/solution.py
+++ b/solution.py
@@ -167,6 +167,8 @@
 MESH = pl.DeviceIdType.MESH
 F32 = jnp.float32
 BF16 = jnp.bfloat16
+PART = jnp.int16
+PART_TOP = 32767.0
 
 
 def fused_kernel(
@@ -175,8 +177,7 @@
     q_ref,
     k_ref,
     v_ref,
-    kpos_ref,
-    qpos_ref,
+    span_ref,
     target_ref,
     wo_hbm,
     resid_ref,
@@ -195,14 +196,19 @@
     square_tp,
     square_ctx,
     norm_all,
+    block,
+    scales,
     part_out,
-    pair_in,
-    far_in,
+    right_in,
+    left_in,
+    step_out,
+    step_in,
     logit,
     pack,
     stat,
     loss_all,
     hidden_grad,
+    hidden_back,
     grad_out,
     grad_in,
     w_sem,
@@ -214,6 +220,8 @@
     cross_sem,
     part_send,
     part_recv,
+    step_send,
+    step_recv,
     stat_sem,
     loss_sem,
     share_send,
@@ -227,13 +235,14 @@
     chips = nc // 2
     mate = chip * 2 + 1 - core
     rows = gl_ref.shape[0]
-    own = rows // tp
+    own = rows // 2
     vocab = gl_ref.shape[1]
     chunks = vocab // chunk
     q_dev = q_ref.shape[0]
     width = gain_ref.shape[1]
     depth = w.shape[0]
     tile = 256
+    back = min(1024, depth)
 
     def remote(src, dst, send, recv, where):
         return pltpu.make_async_remote_copy(
@@ -284,7 +293,19 @@
 
     local_kv = k_ref.shape[1] // HEAD_SIZE
     group = QUERY_HEADS // KEY_VALUE_HEADS
-    visible = kpos_ref[...] <= qpos_ref[...]
+    span_rows, q_span = tok_dev // 2, q_dev // 2
+    lanes = lax.broadcasted_iota(jnp.int32, (group * q_dev, nc * tok_dev), 1)
+    kpos = lanes
+    for i in range(2 * nc):
+        inside = jnp.logical_and(lanes >= i * span_rows, lanes < (i + 1) * span_rows)
+        kpos = jnp.where(inside, lanes + (span_ref[i] - i) * span_rows, kpos)
+    lines = lax.broadcasted_iota(jnp.int32, (group * q_dev, nc * tok_dev), 0)
+    qpos = lines
+    for i in range(2 * group):
+        inside = jnp.logical_and(lines >= i * q_span, lines < (i + 1) * q_span)
+        start = (span_ref[2 * c + i % 2] + 1) * span_rows - q_span - i * q_span
+        qpos = jnp.where(inside, lines + start, qpos)
+    visible = kpos <= qpos
     pieces = []
     for k in range(local_kv):
         lanes = pl.ds(k * HEAD_SIZE, HEAD_SIZE)
@@ -356,193 +377,200 @@
     norm_all[c] = (hidden * scale * gain_ref[...]).astype(BF16)
     gather(norm_all, lambda buf, idx: buf.at[idx], 2)
     for i in range(nc):
-        block_ref[:, i * width : (i + 1) * width] = norm_all[i]
-
-    inner = jnp.logical_or(t == 1, t == 2)
-    pair_mate = t + 1 - 2 * (t % 2)
-    first_far = 2 - 2 * (t // 2)
-    rest = rows - own
-    rest_at = jnp.where(t < 2, own, 0)
-    far_in_rest = jnp.where(t < 2, own, 0)
-    own_in_rest = jnp.where(t < 2, 0, 2 * own)
+        block[:, i * width : (i + 1) * width] = norm_all[i]
+
+    last = tp - 1
+    end = jnp.logical_or(t == 0, t == last)
+    middle = jnp.logical_not(end)
+    side = t // 2
+    low, high = pl.ds(0, own), pl.ds(own, own)
+    own_rows = pl.ds(pl.multiple_of(side * own, 16), own)
 
     def columns_of(j):
         return pl.ds(pl.multiple_of(j * chunk, chunk), chunk)
 
-    def end_copy(j):
-        cols = columns_of(j)
+    def right_sum(j):
         return remote(
-            part_out.at[pl.ds(pl.multiple_of(jnp.where(t < 2, own, 0), 16), rest), cols],
-            pair_in.at[pl.ds(0, rest), cols],
+            part_out.at[low, columns_of(j)],
+            right_in.at[:, columns_of(j)],
             part_send.at[0, j],
             part_recv.at[0, j],
-            (c, pair_mate),
+            (c, jnp.minimum(t + 1, last)),
         )
 
-    def inner_copy(j):
-        cols = columns_of(j)
+    def left_sum(j):
         return remote(
-            part_out.at[pl.ds(pl.multiple_of(pair_mate * own, 16), own), cols],
-            pair_in.at[pl.ds(0, own), cols],
-            part_send.at[0, j],
-            part_recv.at[0, j],
-            (c, pair_mate),
+            part_out.at[high, columns_of(j)],
+            left_in.at[:, columns_of(j)],
+            part_send.at[1, j],
+            part_recv.at[1, j],
+            (c, jnp.maximum(t - 1, 0)),
         )
 
-    def far_copy(j, i):
-        cols = columns_of(j)
-        owner = first_far + i
-        return remote(
-            part_out.at[pl.ds(pl.multiple_of(owner * own, 16), own), cols],
-            far_in.at[:, cols],
-            part_send.at[1 + i, j],
-            part_recv.at[1, j],
-            (c, owner),
-        )
-
-    own_rows = pl.ds(pl.multiple_of(t * own, 16), own)
-
-    @pl.loop(0, chunks)
-    def _(j):
-        w_copy(j).wait()
-
-        @pl.loop(0, chunk // tile)
-        def _(i):
-            cols = pl.ds(pl.multiple_of(j * chunk + i * tile, tile), tile)
-            hidden_grad[:, 0:tile] = jnp.dot(block_ref[...], w[:, cols], preferred_element_type=F32)
-            part_out[:, cols] = hidden_grad[:, 0:tile].astype(BF16)
-            logit[:, cols] = hidden_grad[own_rows, 0:tile]
-
-        @pl.when(inner)
-        def _():
-            inner_copy(j).start()
-
-        @pl.when(jnp.logical_not(inner))
-        def _():
-            end_copy(j).start()
-
-    @pl.when(inner)
-    def _():
-        @pl.loop(0, chunks)
-        def _(j):
-            cols = columns_of(j)
-            end_copy(j).wait_recv()
-            far = pl.ds(pl.multiple_of(first_far * own, 16), 2 * own)
-            total = part_out[far, cols].astype(F32) + pair_in[
-                pl.ds(pl.multiple_of(far_in_rest, 16), 2 * own), cols
-            ].astype(F32)
-            part_out[far, cols] = total.astype(BF16)
-            far_copy(j, 0).start()
-            far_copy(j, 1).start()
-            logit[:, cols] += pair_in[pl.ds(pl.multiple_of(own_in_rest, 16), own), cols].astype(F32)
-
+    def step_copy(j, way):
+        to = jnp.minimum(t + 1, last) if way == 0 else jnp.maximum(t - 1, 0)
+        return remote(step_out.at[way, j], step_in.at[way, j], step_send.at[way, j], step_recv.at[way, j], (c, to))
+
+    def encode(j, way, values):
+        top = jnp.max(jnp.max(jnp.abs(values), axis=1, keepdims=True), axis=0, keepdims=True)
+        top = jnp.maximum(top, 1e-20)
+        coded = jnp.floor(values * (PART_TOP / top) + 0.5).astype(jnp.int32).astype(PART)
+        part_out[low if way == 0 else high, columns_of(j)] = coded
+        step_out[way, j] = jnp.broadcast_to(top / PART_TOP, (8, 128))
+        step_copy(j, way).start()
+        (right_sum if way == 0 else left_sum)(j).start()
+
+    def arrived(j, way):
+        step_copy(j, way).wait_recv()
+        (right_sum if way == 0 else left_sum)(j).wait_recv()
+        coded = (right_in if way == 0 else left_in)[:, columns_of(j)]
+        return coded.astype(jnp.int32).astype(F32) * step_in[way, j][0:1, 0:1]
+
+    def combine(j, way, place):
+        @pl.when(jnp.logical_and(middle, jnp.logical_and(j >= 0, j < chunks)))
+        def _():
+            k = jnp.clip(j, 0, chunks - 1)
+            encode(k, way, logit[place, columns_of(k)] + arrived(k, way))
+
+    lag = 2
+
+    @pl.loop(0, chunks + lag * (tp - 2))
+    def _(step):
+        @pl.when(step < chunks)
+        def _():
+            w_copy(step).wait()
+
+            @pl.loop(0, chunk // tile)
+            def _(i):
+                cols = pl.ds(pl.multiple_of(step * chunk + i * tile, tile), tile)
+                logit[:, cols] = jnp.dot(block[...], w[:, cols], preferred_element_type=F32)
+
+            @pl.when(t == 0)
+            def _():
+                encode(step, 0, logit[high, columns_of(step)])
+
+            @pl.when(t == last)
+            def _():
+                encode(step, 1, logit[low, columns_of(step)])
+
+        combine(step - lag * t, 0, high)
+        combine(step - lag * (last - t), 1, low)
+
+    for i in range(depth // rows):
+        columns = slice(i * rows, (i + 1) * rows)
+        block_ref[columns, :] = block[:, columns].astype(F32).T.astype(BF16)
+
+    scales[...] = jnp.broadcast_to(target_ref[...].astype(F32), (rows, rows)).T
     first_col = c * vocab
-    hits = target_ref[own_rows, :] - first_col
+    hits = scales[own_rows, 0:1].astype(jnp.int32) - first_col
 
     def column_ids(j):
         return lax.broadcasted_iota(jnp.int32, (own, chunk), 1) + j * chunk
+
+    def loss_copy(d):
+        return remote(
+            loss_all.at[side], loss_all.at[side], loss_sem.at[0, d], loss_sem.at[1, side], (c, lax.rem(t + d, tp))
+        )
+
+    def stat_copy(d):
+        return remote(pack, stat.at[c], stat_sem.at[0, d], stat_sem.at[1, d], (lax.rem(c + d, nc), t))
 
     def settle(j, state):
         peak, sums, picked = state
         cols = columns_of(j)
 
-        @pl.when(jnp.logical_not(inner))
-        def _():
-            inner_copy(j).wait_recv()
-            logit[:, cols] += pair_in[0:own, cols].astype(F32)
-
-        far_copy(j, 0).wait_recv()
-        values = logit[:, cols] + far_in[:, cols].astype(F32)
-        logit[:, cols] = values
+        @pl.when(t == 0)
+        def _():
+            logit[low, cols] += arrived(j, 1)
+
+        @pl.when(t == last)
+        def _():
+            logit[high, cols] += arrived(j, 0)
+
+        values = logit[own_rows, cols]
         fresh = jnp.maximum(peak, jnp.max(values, axis=1, keepdims=True))
         sums = sums * jnp.exp(peak - fresh) + jnp.sum(jnp.exp(values - fresh), axis=1, keepdims=True)
         picked = picked + jnp.sum(jnp.where(column_ids(j) == hits, values, 0.0), axis=1, keepdims=True)
         return fresh, sums, picked
 
-    zero = jnp.zeros((own, 1), F32)
-    peak, sums, picked = lax.fori_loop(0, chunks, settle, (zero + MASKED, zero, zero))
-
-    lane = lax.broadcasted_iota(jnp.int32, (own, 128), 1)
-    pack[...] = jnp.where(lane == 0, peak, jnp.where(lane == 1, sums, picked))
-    copies = []
-    for d in range(1, nc):
-        copy = remote(pack, stat.at[c], stat_sem.at[0, d], stat_sem.at[1, d], (lax.rem(c + d, nc), t))
-        copy.start()
-        copies.append(copy)
-    stat[c] = pack[...]
-    for copy in copies:
-        copy.wait()
-    top = stat[0][:, 0:1]
-    for i in range(1, nc):
-        top = jnp.maximum(top, stat[i][:, 0:1])
-    sums, picked = zero, zero
-    for i in range(nc):
-        sums = sums + stat[i][:, 1:2] * jnp.exp(stat[i][:, 0:1] - top)
-        picked = picked + stat[i][:, 2:3]
-    lse = top + jnp.log(sums)
-
-    loss_all[t] = jnp.broadcast_to(jnp.sum(lse - picked, axis=0, keepdims=True), (8, 128))
-    losses = []
-    for d in range(1, tp):
-        copy = remote(
-            loss_all.at[t], loss_all.at[t], loss_sem.at[0, d], loss_sem.at[1, d], (c, lax.rem(t + d, tp))
-        )
-        copy.start()
-        losses.append(copy)
-
-    def share(j, source, step):
-        place = gl_ref.at[pl.ds(pl.multiple_of(source * own, 16), own), columns_of(j)]
-        to = jnp.where(step > 0, jnp.minimum(t + 1, tp - 1), jnp.maximum(t - 1, 0))
-        return remote(
-            place, place, share_send.at[(step > 0) * tp + source, j], share_recv.at[source, j], (c, to)
-        )
-
-    @pl.loop(0, chunks)
-    def _(j):
-        cols = columns_of(j)
-        grads = jnp.exp(logit[:, cols] - lse) - (column_ids(j) == hits).astype(F32)
-        gl_ref[own_rows, cols] = grads.astype(BF16)
-
-        @pl.when(t < tp - 1)
-        def _():
-            share(j, t, 1).start()
-
-        @pl.when(t > 0)
-        def _():
-            share(j, t, 0).start()
-
-    hidden_grad[...] = jnp.zeros_like(hidden_grad)
-
-    @pl.loop(0, chunks)
-    def _(j):
-        for far in range(1, tp):
-
-            @pl.when(t - far >= 0)
-            def _():
-                share(j, t - far, 1).wait_recv()
-
-                @pl.when(t < tp - 1)
-                def _():
-                    share(j, t - far, 1).start()
-
-            @pl.when(t + far < tp)
-            def _():
-                share(j, t + far, 0).wait_recv()
-
-                @pl.when(t > 0)
-                def _():
-                    share(j, t + far, 0).start()
-
-        @pl.loop(0, depth // tile)
+    @pl.when(end)
+    def _():
+        zero = jnp.zeros((own, 1), F32)
+        peak, sums, picked = lax.fori_loop(0, chunks, settle, (zero + MASKED, zero, zero))
+        lane = lax.broadcasted_iota(jnp.int32, (own, 128), 1)
+        pack[...] = jnp.where(lane == 0, peak, jnp.where(lane == 1, sums, picked))
+        for d in range(1, nc):
+            stat_copy(d).start()
+        stat[c] = pack[...]
+        for d in range(1, nc):
+            stat_copy(d).wait()
+        top = stat[0][:, 0:1]
+        for i in range(1, nc):
+            top = jnp.maximum(top, stat[i][:, 0:1])
+        sums, picked = zero, zero
+        for i in range(nc):
+            sums = sums + stat[i][:, 1:2] * jnp.exp(stat[i][:, 0:1] - top)
+            picked = picked + stat[i][:, 2:3]
+        lse = top + jnp.log(sums)
+        loss_all[side] = jnp.broadcast_to(jnp.sum(lse - picked, axis=0, keepdims=True), (8, 128))
+        for d in range(1, tp):
+            loss_copy(d).start()
+        pack[...] = jnp.broadcast_to(lse, (own, 128))
+
+    def share(j, place, to, way):
+        cell = gl_ref.at[place, columns_of(j)]
+        return remote(cell, cell, share_send.at[way, j], share_recv.at[way, j], (c, to))
+
+    def right_share(j):
+        return share(j, low, jnp.minimum(t + 1, last), 0)
+
+    def left_share(j):
+        return share(j, high, jnp.maximum(t - 1, 0), 1)
+
+    hidden_back[...] = jnp.zeros_like(hidden_back)
+
+    def settled(j):
+        @pl.loop(0, depth // back)
         def _(i):
-            cols = pl.ds(pl.multiple_of(i * tile, tile), tile)
-            hidden_grad[:, cols] += lax.dot_general(
+            lines = pl.ds(pl.multiple_of(i * back, back), back)
+            hidden_back[lines, :] += lax.dot_general(
+                w[lines, columns_of(j)],
                 gl_ref[:, columns_of(j)],
-                w[cols, columns_of(j)],
                 (((1,), (1,)), ((), ())),
                 preferred_element_type=F32,
             )
 
+    def relay(j, copy, sends, arrives):
+        live = jnp.logical_and(j >= 0, j < chunks)
+        k = jnp.clip(j, 0, chunks - 1)
+
+        @pl.when(jnp.logical_and(live, arrives))
+        def _():
+            copy(k).wait_recv()
+
+        @pl.when(jnp.logical_and(live, sends))
+        def _():
+            copy(k).start()
+
+    @pl.loop(0, chunks + last)
+    def _(step):
+        @pl.when(jnp.logical_and(end, step < chunks))
+        def _():
+            cols = columns_of(jnp.minimum(step, chunks - 1))
+            grads = jnp.exp(logit[own_rows, cols] - pack[:, 0:1])
+            grads = grads - (column_ids(step) == hits).astype(F32)
+            gl_ref[own_rows, cols] = grads.astype(BF16)
+
+        relay(step - t, right_share, t < last, t > 0)
+        relay(step - (last - t), left_share, t > 0, t < last)
+
+        @pl.when(step >= last)
+        def _():
+            settled(step - last)
+
+    for i in range(depth // rows):
+        columns = slice(i * rows, (i + 1) * rows)
+        hidden_grad[:, columns] = hidden_back[columns, :].T
     grad_out[...] = hidden_grad[...].astype(BF16)
     copies = []
     for d in range(1, nc):
@@ -559,37 +587,36 @@
 
     @pl.loop(0, chunks)
     def _(j):
-        @pl.when(inner)
-        def _():
-            inner_copy(j).wait_send()
-            far_copy(j, 0).wait_send()
-            far_copy(j, 1).wait_send()
-
-        @pl.when(jnp.logical_not(inner))
-        def _():
-            end_copy(j).wait_send()
-
-        @pl.when(t < tp - 1)
-        def _():
-            share(j, t, 1).wait_send()
-            for far in range(1, tp):
-
-                @pl.when(t - far >= 0)
-                def _():
-                    share(j, t - far, 1).wait_send()
+        @pl.when(t < last)
+        def _():
+            step_copy(j, 0).wait_send()
+            right_sum(j).wait_send()
+            right_share(j).wait_send()
 
         @pl.when(t > 0)
         def _():
-            share(j, t, 0).wait_send()
-            for far in range(1, tp):
-
-                @pl.when(t + far < tp)
-                def _():
-                    share(j, t + far, 0).wait_send()
-
-    for copy in losses:
-        copy.wait()
-    loss_ref[...] = (loss_all[0] + loss_all[1] + loss_all[2] + loss_all[3]) / rows
+            step_copy(j, 1).wait_send()
+            left_sum(j).wait_send()
+            left_share(j).wait_send()
+
+    def loss_wait(i):
+        return remote(loss_all.at[i], loss_all.at[i], loss_sem.at[0, 0], loss_sem.at[1, i], (c, lax.rem(t + 1, tp)))
+
+    @pl.when(end)
+    def _():
+        for d in range(1, tp):
+            loss_copy(d).wait_send()
+
+    @pl.when(t != 0)
+    def _():
+        loss_wait(0).wait_recv()
+
+    @pl.when(t != last)
+    def _():
+        loss_wait(1).wait_recv()
+
+    losses_sum = loss_all[0] + loss_all[1]
+    loss_ref[...] = losses_sum[0:1, 0:1] / rows
 
     result = hidden_grad[pl.ds(pl.multiple_of(c * q_dev, 16), q_dev), :]
     for copy in copies:
@@ -613,29 +640,24 @@
     nc, tp = lax.axis_size("ctx"), lax.axis_size("tp")
     tok_dev, kv_width = rotated_keys.shape
     q_dev, q_width = queries.shape
-    span_rows, q_span = tok_dev // 2, q_dev // 2
     rows = q_dev * nc
-    own = rows // tp
+    own = rows // 2
     slice_width = out_weight.shape[3]
     depth, vocab = head_weight.shape
-    chunk = min(1024, vocab)
+    chunk = min(512, vocab)
     chunks = vocab // chunk
-    kpos = slot_positions(span_order, tok_dev * nc, span_rows, span_rows, 0)
-    qpos = slot_positions(span_order, rows, q_span, span_rows, span_rows - q_span)
-    mine = lax.dynamic_slice_in_dim(qpos, lax.axis_index("ctx") * q_dev, q_dev)
-    mine = jnp.tile(mine, QUERY_HEADS // KEY_VALUE_HEADS)[:, None]
     vmem = pl.BlockSpec(memory_space=pltpu.VMEM)
     hbm = pl.BlockSpec(memory_space=pl.ANY)
     dma = pltpu.SemaphoreType.DMA
     loss, grad_normed, block, grad_logits = pl.pallas_call(
         functools.partial(fused_kernel, nc, chunk),
         out_shape=(
-            jax.ShapeDtypeStruct((8, 128), F32),
+            jax.ShapeDtypeStruct((1, 1), F32),
             jax.ShapeDtypeStruct((q_dev, depth), BF16),
-            jax.ShapeDtypeStruct((rows, depth), BF16),
+            jax.ShapeDtypeStruct((depth, rows), BF16),
             jax.ShapeDtypeStruct((rows, vocab), BF16),
         ),
-        in_specs=[vmem] * 6 + [hbm, vmem, vmem, hbm],
+        in_specs=[vmem] * 3 + [pl.BlockSpec(memory_space=pltpu.SMEM), vmem, hbm, vmem, vmem, hbm],
         out_specs=(vmem,) * 4,
         scratch_shapes=[
             pltpu.VMEM((depth, vocab), BF16),
@@ -647,14 +669,19 @@
             pltpu.VMEM((tp, 8, rows), F32),
             pltpu.VMEM((nc, 8, rows), F32),
             pltpu.VMEM((nc, rows, slice_width), BF16),
-            pltpu.VMEM((rows, vocab), BF16),
-            pltpu.VMEM((rows - own, vocab), BF16),
-            pltpu.VMEM((own, vocab), BF16),
-            pltpu.VMEM((own, vocab), F32),
+            pltpu.VMEM((rows, depth), BF16),
+            pltpu.VMEM((rows, rows), F32),
+            pltpu.VMEM((rows, vocab), PART),
+            pltpu.VMEM((own, vocab), PART),
+            pltpu.VMEM((own, vocab), PART),
+            pltpu.VMEM((2, chunks, 8, 128), F32),
+            pltpu.VMEM((2, chunks, 8, 128), F32),
+            pltpu.VMEM((rows, vocab), F32),
             pltpu.VMEM((own, 128), F32),
             pltpu.VMEM((nc, own, 128), F32),
-            pltpu.VMEM((tp, 8, 128), F32),
+            pltpu.VMEM((2, 8, 128), F32),
             pltpu.VMEM((rows, depth), F32),
+            pltpu.VMEM((depth, rows), F32),
             pltpu.VMEM((rows, depth), BF16),
             pltpu.VMEM((nc - 1, q_dev, depth), BF16),
             dma((chunks,)),
@@ -664,12 +691,14 @@
             dma((2, tp - 1)),
             dma((2, tp)),
             dma((2, nc)),
-            dma((3, chunks)),
+            dma((2, chunks)),
+            dma((2, chunks)),
+            dma((2, chunks)),
             dma((2, chunks)),
             dma((2, nc)),
             dma((2, tp)),
-            dma((2 * tp, chunks)),
-            dma((tp, chunks)),
+            dma((2, chunks)),
+            dma((2, chunks)),
             dma((2, nc)),
         ],
         compiler_params=pltpu.CompilerParams(
@@ -679,17 +708,14 @@
         queries,
         rotated_keys,
         value_rows,
-        kpos[None, :],
-        mine,
-        targets[:, None],
+        span_order,
+        targets[None, :],
         out_weight.reshape(q_width, -1),
         residual.reshape(rows, slice_width),
         norm_gain.reshape(1, slice_width),
         head_weight,
     )
-    grad_head = lax.dot_general(
-        block, grad_logits, (((0,), (0,)), ((), ())), preferred_element_type=jnp.float32
-    ).astype(jnp.bfloat16)
+    grad_head = jnp.dot(block, grad_logits, preferred_element_type=F32).astype(BF16)
     return (loss[0, 0], grad_normed, grad_head)
 
 

time: 188 us -> 179 us (0.952)
  Pallas kernels: 160 us -> 154 us
  local copies, waits for them, and re-layouts: 9.23 us -> 5.88 us
  other arithmetic: 2.09 us -> 0 us
    pallas_call x1, Pallas kernels: 160 us -> 154 us  [fused_per_device(): pl.pallas_call(functools.partial(fused_kernel, nc, chunk), out_shape=(jax...]
where the time goes in v2:
time: 179 us
  Pallas kernels  154 us (86%)
  matrix products  16.5 us (9%)
  local copies, waits for them, and re-layouts  5.88 us (3%)
  between operations  2.42 us (1%)
    pallas_call x1, Pallas kernels, fused_per_device(): pl.pallas_call(functools.partial(fused_kernel, nc, chunk), out_shape=(jax...  154 us
    dot_general x1, matrix products, fused_per_device(): jnp.dot(block, grad_logits, preferred_element_type=F32).astype(BF16)  16.5 us
    unnamed x4, local copies, waits for them, and re-layouts  5.88 us

profile of v2, /device:TPU:1, one launch (start us, length us, event | category | flops | bytes accessed | tf_op | source)
XLA Modules:
  0.0 179.0 jit_solution(3011005643193632312)
XLA Ops:
  0.6 5.2 %copy.12 = bf16[256,8,4,256]{3,1,2,0:T(8,128)(2,1)} copy(bf16[256,8,4,256]{3,2,1,0:T(4,128)(2,1)} %bitcast.11) | data formatting | bytes 8388608
  5.9 154.1 %shard_map.112 = (f32[1,1]{1,0:T(1,128)}, bf16[16,2048]{1,0:T(8,128)(2,1)}, bf16[2048,128]{1,0:T(8,128)(2,1)}, bf16[128,8192]{1,0:T(8,128)(2,1)}) custom-call(bf16[16,2048]{1,0:T(8,128)(2,1)} %q_ref.1, bf16[128,256]{1,0:T(8,128)(2,1)} %k_ref.1, bf16[128,256]{1,0:T(8,128)(2,1)} %v_ref.1, s32[16]{0:T(128)} %span_ref.1, s32[1,128]{1,0:T(1,128)} %bitcast.14, ...), custom_call_target="tpu_custom_call" | custom-call | tf_op jit(solution)/shard_map/pallas_call | solution.py:652
  160.0 0.0 copy-start
  160.0 16.5 %convolution_convert_fusion = bf16[2048,8192]{1,0:T(8,128)(2,1)} fusion(bf16[2048,128]{1,0:T(8,128)(2,1)} %get-tuple-element.9, bf16[128,8192]{1,0:T(8,128)(2,1)} %get-tuple-element.10), kind=kOutput, calls=%fused_computation | convolution fusion | flops 4311744512 | bytes 36175872 | tf_op jit(solution)/shard_map/dot_general | solution.py:718
  177.2 0.0 copy-done
  177.2 0.6 copy.16
Async XLA Ops:
  160.0 17.2 %copy-start = (bf16[16,2048]{1,0:T(8,128)(2,1)S(1)}, bf16[16,2048]{1,0:T(8,128)(2,1)}, u32[]{:S(2)}) copy-start(bf16[16,2048]{1,0:T(8,128)(2,1)} %get-tuple-element.15) | copy-start | bytes 196612
